TPU v7x, 512 devices: a whole 4x4x16 slice. The times are simulated.
512 devices in a mesh: ctx: 128 (over z, y, core), head: 4 (over x).
Axes of the slice: x: 4, y: 4, z: 16, core: 2. Of those that a mesh axis runs over, the one named last changes fastest.
Arguments:
- queries: bfloat16 [32768, 12288], P(('ctx', 'head')), may hold values from -96 to 96
- key_rows: bfloat16 [32768, 768], P(('ctx', 'head')), may hold values from -8 to 8
- values: bfloat16 [32768, 512], P(('ctx', 'head')), may hold values from -6 to 6
- gate_logits: bfloat16 [32768, 128], P(('ctx', 'head')), may hold values from -6 to 6
- key_mix: bfloat16 [4, 32, 192], replicated, may hold values from -1 to 1
- key_proj: bfloat16 [4, 192, 192], replicated, may hold values from -1 to 1
- value_mix: bfloat16 [4, 32, 128], replicated, may hold values from -1 to 1
- value_proj: bfloat16 [4, 128, 128], replicated, may hold values from -0.5 to 0.5
Outputs:
- mixture: bfloat16 [32768, 8192], P(('ctx', 'head'))
All inputs are finite; a program needn't handle non-finite values.
Results may differ from a plain program's by a relative error of at most 0.012.
Values may be sent and summed in bfloat16 or wider, within the bound.
A program may use at most 64 MiB of HBM per device.

v0:
```python
import math
import jax
import jax.numpy as jnp
from jax import lax
from jax.sharding import PartitionSpec as P

QHEADS = 64
GROUPS = 4
KDIM = 192
VDIM = 128
BLOCK = 32
STRIDE = 16
WINDOW = 512


def passed_along(value, axis, steps):
    count = lax.axis_size(axis)
    leading, last = (max(0, -steps), min(count, count - steps))
    return lax.ppermute(value, axis, [(source, source + steps) for source in range(leading, last)])


def compress_block(rows, mixer, projection):
    block_count = rows.shape[0] // STRIDE - 1
    halves = rows.reshape(block_count + 1, STRIDE, rows.shape[1], rows.shape[2])
    pooled = jnp.einsum(
        "bjgd,gjd->bgd", halves[:-1], mixer[:, :STRIDE], preferred_element_type=jnp.float32
    )
    pooled = pooled + jnp.einsum(
        "bjgd,gjd->bgd", halves[1:], mixer[:, STRIDE:], preferred_element_type=jnp.float32
    )
    summary = jnp.einsum(
        "bgd,gde->bge", pooled.astype(jnp.bfloat16), projection, preferred_element_type=jnp.float32
    )
    return summary.astype(jnp.bfloat16)


def soft_mix(scores, visible, value_rows):
    masked = jnp.where(visible, scores, -1e30)
    highest = jnp.max(masked, axis=-1, keepdims=True)
    weights = jnp.where(visible, jnp.exp(scores - highest), 0.0)
    weight_total = jnp.sum(weights, axis=-1)
    numerator = jnp.einsum(
        "tghs,sgd->tghd",
        weights.astype(jnp.bfloat16),
        value_rows,
        preferred_element_type=jnp.float32,
    )
    safe_total = jnp.where(weight_total > 0.0, weight_total, 1.0)
    return numerator / safe_total[..., None]


def attend(
    query_rows,
    own_keys,
    own_values,
    gate_rows,
    key_mix,
    key_proj,
    value_mix,
    value_proj,
    group_count,
    query_offset,
):
    per_group = QHEADS // GROUPS
    row_count = query_rows.shape[0]
    block_rows = own_keys.shape[0]
    score_scale = 1.0 / math.sqrt(KDIM)
    queried = query_rows.reshape(row_count, group_count, per_group, KDIM)
    block_keys = own_keys.reshape(block_rows, group_count, KDIM)
    block_values = own_values.reshape(block_rows, group_count, VDIM)
    block_first = lax.axis_index("ctx") * block_rows
    positions = block_first + query_offset + jnp.arange(row_count, dtype=jnp.int32)
    next_keys, next_values = passed_along((block_keys[:STRIDE], block_values[:STRIDE]), "ctx", -1)
    summary_keys = compress_block(jnp.concatenate([block_keys, next_keys], 0), key_mix, key_proj)
    summary_values = compress_block(
        jnp.concatenate([block_values, next_values], 0), value_mix, value_proj
    )
    distance_count = -(-WINDOW // block_rows)
    near_keys = []
    near_values = []
    for distance in range(distance_count, 0, -1):
        far_keys, far_values = passed_along((block_keys, block_values), "ctx", distance)
        near_keys.append(far_keys)
        near_values.append(far_values)
    near_keys.append(block_keys)
    near_values.append(block_values)
    near_keys = jnp.concatenate(near_keys, 0)
    near_values = jnp.concatenate(near_values, 0)
    key_places = (
        block_first - distance_count * block_rows + jnp.arange(near_keys.shape[0], dtype=jnp.int32)
    )
    near_visible = (
        (key_places[None, :] <= positions[:, None])
        & (key_places[None, :] > positions[:, None] - WINDOW)
        & (key_places[None, :] >= 0)
    )
    scores = (
        jnp.einsum("tghd,sgd->tghs", queried, near_keys, preferred_element_type=jnp.float32)
        * score_scale
    )
    window_out = soft_mix(scores, near_visible[:, None, None, :], near_values)

    def absorb_part(running, portion, offset):
        part_keys, part_values = portion
        block_ends = (offset + jnp.arange(part_keys.shape[0], dtype=jnp.int32)) * STRIDE + BLOCK - 1
        visible = (block_ends[None, :] <= positions[:, None])[:, None, None, :]
        highest, weight_total, numerator = running
        part_scores = (
            jnp.einsum("tghd,bgd->tghb", queried, part_keys, preferred_element_type=jnp.float32)
            * score_scale
        )
        masked = jnp.where(visible, part_scores, -1e30)
        new_highest = jnp.maximum(highest, jnp.max(masked, axis=-1))
        weights = jnp.where(visible, jnp.exp(part_scores - new_highest[..., None]), 0.0)
        factor = jnp.exp(highest - new_highest)
        weight_total = weight_total * factor + jnp.sum(weights, axis=-1)
        numerator = numerator * factor[..., None] + jnp.einsum(
            "tghb,bgd->tghd",
            weights.astype(jnp.bfloat16),
            part_values,
            preferred_element_type=jnp.float32,
        )
        return (new_highest, weight_total, numerator)

    initial = (
        jnp.full((row_count, group_count, per_group), -1e30, jnp.float32),
        jnp.zeros((row_count, group_count, per_group), jnp.float32),
        jnp.zeros((row_count, group_count, per_group, VDIM), jnp.float32),
    )
    portion = (
        lax.all_gather(summary_keys, "ctx", axis=0, tiled=True),
        lax.all_gather(summary_values, "ctx", axis=0, tiled=True),
    )
    part_count = portion[0].shape[0]

    def step(step_index, state):
        sub_keys = lax.dynamic_slice_in_dim(portion[0], step_index * 256, 256, 0)
        sub_values = lax.dynamic_slice_in_dim(portion[1], step_index * 256, 256, 0)
        return absorb_part(state, (sub_keys, sub_values), step_index * 256)

    highest, weight_total, numerator = lax.fori_loop(0, part_count // 256, step, initial)
    compressed_out = numerator / jnp.where(weight_total > 0.0, weight_total, 1.0)[..., None]
    gate_values = jax.nn.sigmoid(
        gate_rows.reshape(row_count, group_count, per_group, 2).astype(jnp.float32)
    )
    mixture = gate_values[..., 0:1] * compressed_out + gate_values[..., 1:2] * window_out
    return mixture.astype(jnp.bfloat16).reshape(row_count, group_count * per_group * VDIM)


def local(queries, key_rows, values, gate_logits, key_mix, key_proj, value_mix, value_proj):
    query_rows, own_keys, own_values, gate_rows = (
        lax.all_to_all(queries, "head", split_axis=1, concat_axis=0, tiled=True),
        lax.all_to_all(key_rows, "head", split_axis=1, concat_axis=0, tiled=True),
        lax.all_to_all(values, "head", split_axis=1, concat_axis=0, tiled=True),
        lax.all_to_all(gate_logits, "head", split_axis=1, concat_axis=0, tiled=True),
    )
    group_index = lax.axis_index("head")
    key_mix = lax.dynamic_slice_in_dim(key_mix, group_index, 1, 0)
    key_proj = lax.dynamic_slice_in_dim(key_proj, group_index, 1, 0)
    value_mix = lax.dynamic_slice_in_dim(value_mix, group_index, 1, 0)
    value_proj = lax.dynamic_slice_in_dim(value_proj, group_index, 1, 0)
    group_count = 1
    query_offset = 0
    mixture = attend(
        query_rows,
        own_keys,
        own_values,
        gate_rows,
        key_mix,
        key_proj,
        value_mix,
        value_proj,
        group_count,
        query_offset,
    )
    return lax.all_to_all(mixture, "head", split_axis=0, concat_axis=1, tiled=True)


def solution(mesh):
    placed = (
        P(("ctx", "head"), None),
        P(("ctx", "head"), None),
        P(("ctx", "head"), None),
        P(("ctx", "head"), None),
        P(),
        P(),
        P(),
        P(),
    )
    return jax.shard_map(
        local, mesh=mesh, in_specs=placed, out_specs=P(("ctx", "head"), None), check_vma=False
    )
```

profile of v0, /device:TPU:1, one launch (start us, length us, event | category | flops | bytes accessed | tf_op | source)
XLA Modules:
  0.0 378.0 jit_solution(15518361057223146056)
XLA Ops:
  0.0 0.9 copy.55
  0.9 0.7 reshape.421
  1.6 4.8 %all-to-all-start = ((bf16[4,2,1024]{2,1,0:T(2,128)(2,1)}), bf16[4,2,1024]{2,1,0:T(2,128)(2,1)S(1)}, u32[]{:S(2)}, u32[]{:S(2)}) async-start(bf16[4,2,1024]{2,1,0:T(2,128)(2,1)} %reshape.421), calls=%async_computation | async-start | bytes 32768 | tf_op jit(solution)/shard_map/all_to_all | solution.py:155
  6.5 1.5 copy_bitcast_fusion.1
  7.9 0.7 fusion.61
  8.6 1.0 and_and_fusion
  9.6 0.7 fusion.63
  10.3 1.1 all_to_all.62
  11.4 0.7 copy.57
  12.0 2.7 copy.125
  14.7 4.2 %all-to-all-start.3 = ((bf16[64,4,128]{2,0,1:T(8,128)(2,1)}), bf16[64,4,128]{2,0,1:T(8,128)(2,1)S(1)}, u32[]{:S(2)}, u32[]{:S(2)}) async-start(bf16[64,4,128]{2,0,1:T(8,128)(2,1)} %copy_bitcast_fusion.1), calls=%async_computation.3 | async-start | bytes 131072 | tf_op jit(solution)/shard_map/all_to_all | solution.py:154
  19.3 4.2 %all-to-all-done.3 = bf16[64,4,128]{2,0,1:T(8,128)(2,1)S(1)} async-done(((bf16[64,4,128]{2,0,1:T(8,128)(2,1)}), bf16[64,4,128]{2,0,1:T(8,128)(2,1)S(1)}, u32[]{:S(2)}, u32[]{:S(2)}) %all-to-all-start.3) | async-done | bytes 65568 | tf_op jit(solution)/shard_map/all_to_all | solution.py:154
  23.4 3.3 all-to-all-start.1
  26.8 0.6 copy_bitcast_fusion.2
  27.4 0.7 copy.63
  28.1 3.8 %collective-permute-start.2 = (bf16[256,1,128]{0,2,1:T(8,128)(2,1)}, bf16[256,1,128]{0,2,1:T(8,128)(2,1)}, u32[]{:S(2)}, u32[]{:S(2)}) collective-permute-start(bf16[256,1,128]{0,2,1:T(8,128)(2,1)} %copy.63), channel_id=1, source_target_pairs={{0,8},{4,12},{8,16},{12,20},{16,24},{20,28},{24,32},{28,36},{32,40... | collective-permute-start | bytes 196616 | tf_op jit(solution)/shard_map/ppermute | solution.py:19
  31.9 5.4 %collective-permute-start.3 = (bf16[256,1,128]{0,2,1:T(8,128)(2,1)}, bf16[256,1,128]{0,2,1:T(8,128)(2,1)}, u32[]{:S(2)}, u32[]{:S(2)}) collective-permute-start(bf16[256,1,128]{0,2,1:T(8,128)(2,1)} %copy.63), channel_id=1, source_target_pairs={{0,4},{4,8},{8,12},{12,16},{16,20},{20,24},{24,28},{28,32},{32,36}... | collective-permute-start | bytes 196616 | tf_op jit(solution)/shard_map/ppermute | solution.py:19
  37.3 3.4 collective-permute-start.1
  40.8 4.5 %all-to-all-start.2 = ((bf16[64,4,3072]{2,0,1:T(8,128)(2,1)}), bf16[64,4,3072]{2,0,1:T(8,128)(2,1)}, u32[]{:S(2)}, u32[]{:S(2)}) async-start(bf16[64,4,3072]{2,0,1:T(8,128)(2,1)} %bitcast.225), calls=%async_computation.2 | async-start | bytes 3145728 | tf_op jit(solution)/shard_map/all_to_all | solution.py:152
  45.6 0.9 fusion.43
  46.5 96.4 %all_gather.7 = bf16[2048,1,128]{2,0,1:T(8,128)(2,1)} all-gather(bf16[16,1,128]{2,0,1:T(8,128)(2,1)S(1)} %fusion.43), channel_id=1, replica_groups=mesh['ctx'=128,'head'=4] {'ctx'}, dimensions={0}, use_global_device_ids=true | all-gather | bytes 528384 | tf_op jit(solution)/shard_map/all_gather | solution.py:132
  142.9 0.7 copy.66
  143.6 2.1 collective-permute-start.4
  145.7 2.9 collective-permute-start.5
  148.5 2.1 collective-permute-start
  150.8 2.7 collective-permute-done
  153.7 0.2 fusion.42
  153.9 102.0 %all_gather.6 = bf16[2048,1,192]{2,0,1:T(8,128)(2,1)S(1)} all-gather(bf16[16,1,192]{2,0,1:T(8,128)(2,1)S(1)} %fusion.42), channel_id=1, replica_groups=mesh['ctx'=128,'head'=4] {'ctx'}, dimensions={0}, use_global_device_ids=true | all-gather | bytes 792576 | tf_op jit(solution)/shard_map/all_gather | solution.py:131
  255.9 1.3 copy.60
  257.3 4.7 %reshape.391 = bf16[256,1,16,192]{3,2,0,1:T(8,128)(2,1)} reshape(bf16[4,64,3072]{2,1,0:T(8,128)(2,1)} %bitcast.28) | data formatting | bytes 3145728 | tf_op jit(solution)/shard_map/reshape | solution.py:68
  262.0 4.4 %copy.61 = bf16[256,1,16,192]{0,3,2,1:T(8,128)(2,1)} copy(bf16[256,1,16,192]{3,2,0,1:T(8,128)(2,1)} %reshape.391) | data formatting | bytes 3145728
  266.4 73.6 %while.22 = (s32[]{:T(128)}, f32[256,1,16]{0,2,1:T(8,128)S(1)}, f32[256,1,16]{0,2,1:T(8,128)S(1)}, f32[256,1,16,128]{0,3,2,1:T(8,128)S(1)}, bf16[2048,1,192]{0,2...) while((s32[]{:T(128)}, f32[256,1,16]{0,2,1:T(8,128)S(1)}, ...), condition=%wide.region_3.4_spmd.clone, body=%wide.region_0.3_spmd.clone.sunk | while | flops 684286976 | bytes 35819736 | solution.py:141
  266.5 4.3 %fusion.80 = (f32[256,16]{0,1:T(8,128)S(1)}, f32[256,256,16]{1,0,2:T(8,128)}) fusion(pred[256,256]{0,1:T(8,128)(4,1)S(1)} %broadcast_compare_fusion.3, bf16[256,1,16,192]{0,3,2,1:T(8,128)(2,1)} %get-tuple-element.451, bf16[2048,1,192]{0,2,1:T(8,128)(2,1)} %get-tuple-element.450, s32[]{:T(128)S(6)} %select_n.112), kind=kOutput, calls=%fused_computation.3.clone.1 | convolution fusion | flops 405794816 | bytes 5947396 | tf_op jit(solution)/shard_map/while/body/eval_jaxpr/tghd,bgd->tghb/dot_general | solution.py:109
  270.9 3.8 %bitcast_add_fusion.6 = f32[256,1,16,128]{0,3,2,1:T(8,128)S(1)} fusion(f32[256,1,16,128]{0,3,2,1:T(8,128)S(1)} %get-tuple-element.437, f32[256,256,16]{1,0,2:T(8,128)} %get-tuple-element.420, f32[256,16]{0,1:T(8,128)S(1)} %bitcast.223, pred[256,256]{0,1:T(8,128)(4,1)S(1)} %broadcast_compare_fusion.3, f32[256,16]{0,1:T(8,128)S(1)} %get-tuple-element.421, ...), kind=kOutput, calls=%fused_computation.10.clone.1 | convolution fusion | flops 274202624 | bytes 8552453 | tf_op jit(solution)/shard_map/while/body/eval_jaxpr/tghb,bgd->tghd/dot_general | solution.py:117
  274.7 0.9 fusion.82
  275.8 4.3 %fusion.80 = (f32[256,16]{0,1:T(8,128)S(1)}, f32[256,256,16]{1,0,2:T(8,128)}) fusion(pred[256,256]{0,1:T(8,128)(4,1)S(1)} %broadcast_compare_fusion.3, bf16[256,1,16,192]{0,3,2,1:T(8,128)(2,1)} %get-tuple-element.451, bf16[2048,1,192]{0,2,1:T(8,128)(2,1)} %get-tuple-element.450, s32[]{:T(128)S(6)} %select_n.112), kind=kOutput, calls=%fused_computation.3.clone.1 | convolution fusion | flops 405794816 | bytes 5947396 | tf_op jit(solution)/shard_map/while/body/eval_jaxpr/tghd,bgd->tghb/dot_general | solution.py:109
  280.1 3.8 %bitcast_add_fusion.6 = f32[256,1,16,128]{0,3,2,1:T(8,128)S(1)} fusion(f32[256,1,16,128]{0,3,2,1:T(8,128)S(1)} %get-tuple-element.437, f32[256,256,16]{1,0,2:T(8,128)} %get-tuple-element.420, f32[256,16]{0,1:T(8,128)S(1)} %bitcast.223, pred[256,256]{0,1:T(8,128)(4,1)S(1)} %broadcast_compare_fusion.3, f32[256,16]{0,1:T(8,128)S(1)} %get-tuple-element.421, ...), kind=kOutput, calls=%fused_computation.10.clone.1 | convolution fusion | flops 274202624 | bytes 8552453 | tf_op jit(solution)/shard_map/while/body/eval_jaxpr/tghb,bgd->tghd/dot_general | solution.py:117
  283.9 0.9 fusion.82
  285.0 4.3 %fusion.80 = (f32[256,16]{0,1:T(8,128)S(1)}, f32[256,256,16]{1,0,2:T(8,128)}) fusion(pred[256,256]{0,1:T(8,128)(4,1)S(1)} %broadcast_compare_fusion.3, bf16[256,1,16,192]{0,3,2,1:T(8,128)(2,1)} %get-tuple-element.451, bf16[2048,1,192]{0,2,1:T(8,128)(2,1)} %get-tuple-element.450, s32[]{:T(128)S(6)} %select_n.112), kind=kOutput, calls=%fused_computation.3.clone.1 | convolution fusion | flops 405794816 | bytes 5947396 | tf_op jit(solution)/shard_map/while/body/eval_jaxpr/tghd,bgd->tghb/dot_general | solution.py:109
  289.3 3.8 %bitcast_add_fusion.6 = f32[256,1,16,128]{0,3,2,1:T(8,128)S(1)} fusion(f32[256,1,16,128]{0,3,2,1:T(8,128)S(1)} %get-tuple-element.437, f32[256,256,16]{1,0,2:T(8,128)} %get-tuple-element.420, f32[256,16]{0,1:T(8,128)S(1)} %bitcast.223, pred[256,256]{0,1:T(8,128)(4,1)S(1)} %broadcast_compare_fusion.3, f32[256,16]{0,1:T(8,128)S(1)} %get-tuple-element.421, ...), kind=kOutput, calls=%fused_computation.10.clone.1 | convolution fusion | flops 274202624 | bytes 8552453 | tf_op jit(solution)/shard_map/while/body/eval_jaxpr/tghb,bgd->tghd/dot_general | solution.py:117
  293.1 0.9 fusion.82
  294.2 4.3 %fusion.80 = (f32[256,16]{0,1:T(8,128)S(1)}, f32[256,256,16]{1,0,2:T(8,128)}) fusion(pred[256,256]{0,1:T(8,128)(4,1)S(1)} %broadcast_compare_fusion.3, bf16[256,1,16,192]{0,3,2,1:T(8,128)(2,1)} %get-tuple-element.451, bf16[2048,1,192]{0,2,1:T(8,128)(2,1)} %get-tuple-element.450, s32[]{:T(128)S(6)} %select_n.112), kind=kOutput, calls=%fused_computation.3.clone.1 | convolution fusion | flops 405794816 | bytes 5947396 | tf_op jit(solution)/shard_map/while/body/eval_jaxpr/tghd,bgd->tghb/dot_general | solution.py:109
  298.5 3.8 %bitcast_add_fusion.6 = f32[256,1,16,128]{0,3,2,1:T(8,128)S(1)} fusion(f32[256,1,16,128]{0,3,2,1:T(8,128)S(1)} %get-tuple-element.437, f32[256,256,16]{1,0,2:T(8,128)} %get-tuple-element.420, f32[256,16]{0,1:T(8,128)S(1)} %bitcast.223, pred[256,256]{0,1:T(8,128)(4,1)S(1)} %broadcast_compare_fusion.3, f32[256,16]{0,1:T(8,128)S(1)} %get-tuple-element.421, ...), kind=kOutput, calls=%fused_computation.10.clone.1 | convolution fusion | flops 274202624 | bytes 8552453 | tf_op jit(solution)/shard_map/while/body/eval_jaxpr/tghb,bgd->tghd/dot_general | solution.py:117
  302.3 0.9 fusion.82
  303.4 4.3 %fusion.80 = (f32[256,16]{0,1:T(8,128)S(1)}, f32[256,256,16]{1,0,2:T(8,128)}) fusion(pred[256,256]{0,1:T(8,128)(4,1)S(1)} %broadcast_compare_fusion.3, bf16[256,1,16,192]{0,3,2,1:T(8,128)(2,1)} %get-tuple-element.451, bf16[2048,1,192]{0,2,1:T(8,128)(2,1)} %get-tuple-element.450, s32[]{:T(128)S(6)} %select_n.112), kind=kOutput, calls=%fused_computation.3.clone.1 | convolution fusion | flops 405794816 | bytes 5947396 | tf_op jit(solution)/shard_map/while/body/eval_jaxpr/tghd,bgd->tghb/dot_general | solution.py:109
  307.7 3.8 %bitcast_add_fusion.6 = f32[256,1,16,128]{0,3,2,1:T(8,128)S(1)} fusion(f32[256,1,16,128]{0,3,2,1:T(8,128)S(1)} %get-tuple-element.437, f32[256,256,16]{1,0,2:T(8,128)} %get-tuple-element.420, f32[256,16]{0,1:T(8,128)S(1)} %bitcast.223, pred[256,256]{0,1:T(8,128)(4,1)S(1)} %broadcast_compare_fusion.3, f32[256,16]{0,1:T(8,128)S(1)} %get-tuple-element.421, ...), kind=kOutput, calls=%fused_computation.10.clone.1 | convolution fusion | flops 274202624 | bytes 8552453 | tf_op jit(solution)/shard_map/while/body/eval_jaxpr/tghb,bgd->tghd/dot_general | solution.py:117
  311.5 0.9 fusion.82
  312.6 4.3 %fusion.80 = (f32[256,16]{0,1:T(8,128)S(1)}, f32[256,256,16]{1,0,2:T(8,128)}) fusion(pred[256,256]{0,1:T(8,128)(4,1)S(1)} %broadcast_compare_fusion.3, bf16[256,1,16,192]{0,3,2,1:T(8,128)(2,1)} %get-tuple-element.451, bf16[2048,1,192]{0,2,1:T(8,128)(2,1)} %get-tuple-element.450, s32[]{:T(128)S(6)} %select_n.112), kind=kOutput, calls=%fused_computation.3.clone.1 | convolution fusion | flops 405794816 | bytes 5947396 | tf_op jit(solution)/shard_map/while/body/eval_jaxpr/tghd,bgd->tghb/dot_general | solution.py:109
  316.9 3.8 %bitcast_add_fusion.6 = f32[256,1,16,128]{0,3,2,1:T(8,128)S(1)} fusion(f32[256,1,16,128]{0,3,2,1:T(8,128)S(1)} %get-tuple-element.437, f32[256,256,16]{1,0,2:T(8,128)} %get-tuple-element.420, f32[256,16]{0,1:T(8,128)S(1)} %bitcast.223, pred[256,256]{0,1:T(8,128)(4,1)S(1)} %broadcast_compare_fusion.3, f32[256,16]{0,1:T(8,128)S(1)} %get-tuple-element.421, ...), kind=kOutput, calls=%fused_computation.10.clone.1 | convolution fusion | flops 274202624 | bytes 8552453 | tf_op jit(solution)/shard_map/while/body/eval_jaxpr/tghb,bgd->tghd/dot_general | solution.py:117
  320.7 0.9 fusion.82
  321.8 4.3 %fusion.80 = (f32[256,16]{0,1:T(8,128)S(1)}, f32[256,256,16]{1,0,2:T(8,128)}) fusion(pred[256,256]{0,1:T(8,128)(4,1)S(1)} %broadcast_compare_fusion.3, bf16[256,1,16,192]{0,3,2,1:T(8,128)(2,1)} %get-tuple-element.451, bf16[2048,1,192]{0,2,1:T(8,128)(2,1)} %get-tuple-element.450, s32[]{:T(128)S(6)} %select_n.112), kind=kOutput, calls=%fused_computation.3.clone.1 | convolution fusion | flops 405794816 | bytes 5947396 | tf_op jit(solution)/shard_map/while/body/eval_jaxpr/tghd,bgd->tghb/dot_general | solution.py:109
  326.1 3.8 %bitcast_add_fusion.6 = f32[256,1,16,128]{0,3,2,1:T(8,128)S(1)} fusion(f32[256,1,16,128]{0,3,2,1:T(8,128)S(1)} %get-tuple-element.437, f32[256,256,16]{1,0,2:T(8,128)} %get-tuple-element.420, f32[256,16]{0,1:T(8,128)S(1)} %bitcast.223, pred[256,256]{0,1:T(8,128)(4,1)S(1)} %broadcast_compare_fusion.3, f32[256,16]{0,1:T(8,128)S(1)} %get-tuple-element.421, ...), kind=kOutput, calls=%fused_computation.10.clone.1 | convolution fusion | flops 274202624 | bytes 8552453 | tf_op jit(solution)/shard_map/while/body/eval_jaxpr/tghb,bgd->tghd/dot_general | solution.py:117
  329.9 0.9 fusion.82
  331.0 4.3 %fusion.80 = (f32[256,16]{0,1:T(8,128)S(1)}, f32[256,256,16]{1,0,2:T(8,128)}) fusion(pred[256,256]{0,1:T(8,128)(4,1)S(1)} %broadcast_compare_fusion.3, bf16[256,1,16,192]{0,3,2,1:T(8,128)(2,1)} %get-tuple-element.451, bf16[2048,1,192]{0,2,1:T(8,128)(2,1)} %get-tuple-element.450, s32[]{:T(128)S(6)} %select_n.112), kind=kOutput, calls=%fused_computation.3.clone.1 | convolution fusion | flops 405794816 | bytes 5947396 | tf_op jit(solution)/shard_map/while/body/eval_jaxpr/tghd,bgd->tghb/dot_general | solution.py:109
  335.3 3.8 %bitcast_add_fusion.6 = f32[256,1,16,128]{0,3,2,1:T(8,128)S(1)} fusion(f32[256,1,16,128]{0,3,2,1:T(8,128)S(1)} %get-tuple-element.437, f32[256,256,16]{1,0,2:T(8,128)} %get-tuple-element.420, f32[256,16]{0,1:T(8,128)S(1)} %bitcast.223, pred[256,256]{0,1:T(8,128)(4,1)S(1)} %broadcast_compare_fusion.3, f32[256,16]{0,1:T(8,128)S(1)} %get-tuple-element.421, ...), kind=kOutput, calls=%fused_computation.10.clone.1 | convolution fusion | flops 274202624 | bytes 8552453 | tf_op jit(solution)/shard_map/while/body/eval_jaxpr/tghb,bgd->tghd/dot_general | solution.py:117
  339.1 0.9 fusion.82
  340.1 4.7 %reshape.401 = bf16[256,16,192]{2,1,0:T(8,128)(2,1)} reshape(bf16[4,64,3072]{2,1,0:T(8,128)(2,1)} %bitcast.28) | data formatting | bytes 3145728 | tf_op jit(solution)/shard_map/reshape.38
  344.8 4.7 %fusion.27 = (f32[256,16]{0,1:T(8,128)S(1)}, f32[768,256,16]{1,0,2:T(8,128)S(1)}) fusion(pred[256,768]{0,1:T(8,128)(4,1)S(1)} %copy-done.2, bf16[256,16,192]{2,1,0:T(8,128)(2,1)} %reshape.401, bf16[256,1,192]{0,2,1:T(8,128)(2,1)} %copy.66, bf16[256,1,192]{0,2,1:T(8,128)(2,1)} %collective-permute-done.5, bf16[256,1,192]{0,2,1:T(8,128)(2,1)} %collective-permute-done.4), kind=kOutput, calls=%fused_computation.36 | convolution fusion | flops 1218277376 | bytes 14663680 | tf_op jit(solution)/shard_map/tghd,sgd->tghs/dot_general | solution.py:98
  349.5 2.5 fusion.30
  352.1 3.9 %fusion.36 = bf16[256,1,16,128]{0,3,2,1:T(8,128)(2,1)S(1)} fusion(f32[256,1,16,128]{0,3,2,1:T(8,128)S(1)} %get-tuple-element.263, f32[768,256,16]{1,0,2:T(8,128)S(1)} %get-tuple-element.356, f32[256,16]{0,1:T(8,128)S(1)} %get-tuple-element.355, pred[256,768]{0,1:T(8,128)(4,1)S(1)} %copy-done.3, f32[256,16]{0,1:T(8,128)S(1)} %compare_select_fusion, ...), kind=kOutput, calls=%fused_computation.45 | convolution fusion | flops 821624832 | bytes 16203776 | tf_op jit(solution)/shard_map/tghs,sgd->tghd/dot_general | solution.py:42
  356.1 1.1 copy.71
  357.2 0.5 all_to_all.71
  357.7 19.2 %all_to_all.80 = bf16[4,64,2048]{2,1,0:T(8,128)(2,1)S(1)} all-to-all(bf16[4,64,2048]{2,1,0:T(8,128)(2,1)S(1)} %all_to_all.71), channel_id=1, replica_groups=mesh['ctx'=128,'head'=4] {'head'}, dimensions={0} | all-to-all | bytes 2097152 | tf_op jit(solution)/shard_map/all_to_all | solution.py:176
  376.9 1.1 copy.116
  (101 shorter events, 2.1 us)
Async XLA Ops:
  0.0 153.7 %copy-start = (bf16[4,192,192]{2,1,0:T(8,128)(2,1)S(1)}, bf16[4,192,192]{2,1,0:T(8,128)(2,1)}, u32[]{:S(2)}) copy-start(bf16[4,192,192]{2,1,0:T(8,128)(2,1)} %param.15) | copy-start | bytes 884740
  1.6 13.1 %all-to-all-start = ((bf16[4,2,1024]{2,1,0:T(2,128)(2,1)}), bf16[4,2,1024]{2,1,0:T(2,128)(2,1)S(1)}, u32[]{:S(2)}, u32[]{:S(2)}) async-start(bf16[4,2,1024]{2,1,0:T(2,128)(2,1)} %reshape.421), calls=%async_computation | async-start | bytes 32768 | tf_op jit(solution)/shard_map/all_to_all | solution.py:155
  14.7 8.7 %all-to-all-start.3 = ((bf16[64,4,128]{2,0,1:T(8,128)(2,1)}), bf16[64,4,128]{2,0,1:T(8,128)(2,1)S(1)}, u32[]{:S(2)}, u32[]{:S(2)}) async-start(bf16[64,4,128]{2,0,1:T(8,128)(2,1)} %copy_bitcast_fusion.1), calls=%async_computation.3 | async-start | bytes 131072 | tf_op jit(solution)/shard_map/all_to_all | solution.py:154
  23.4 17.3 %all-to-all-start.1 = ((bf16[64,4,192]{2,0,1:T(8,128)(2,1)}), bf16[64,4,192]{2,0,1:T(8,128)(2,1)S(1)}, u32[]{:S(2)}, u32[]{:S(2)}) async-start(bf16[64,4,192]{2,0,1:T(8,128)(2,1)} %copy.57), calls=%async_computation.1 | async-start | bytes 262144 | tf_op jit(solution)/shard_map/all_to_all | solution.py:153
  28.1 324.0 %collective-permute-start.2 = (bf16[256,1,128]{0,2,1:T(8,128)(2,1)}, bf16[256,1,128]{0,2,1:T(8,128)(2,1)}, u32[]{:S(2)}, u32[]{:S(2)}) collective-permute-start(bf16[256,1,128]{0,2,1:T(8,128)(2,1)} %copy.63), channel_id=1, source_target_pairs={{0,8},{4,12},{8,16},{12,20},{16,24},{20,28},{24,32},{28,36},{32,40... | collective-permute-start | bytes 196616 | tf_op jit(solution)/shard_map/ppermute | solution.py:19
  31.9 320.2 %collective-permute-start.3 = (bf16[256,1,128]{0,2,1:T(8,128)(2,1)}, bf16[256,1,128]{0,2,1:T(8,128)(2,1)}, u32[]{:S(2)}, u32[]{:S(2)}) collective-permute-start(bf16[256,1,128]{0,2,1:T(8,128)(2,1)} %copy.63), channel_id=1, source_target_pairs={{0,4},{4,8},{8,12},{12,16},{16,20},{20,24},{24,28},{28,32},{32,36}... | collective-permute-start | bytes 196616 | tf_op jit(solution)/shard_map/ppermute | solution.py:19
  37.3 8.1 %collective-permute-start.1 = (bf16[16,1,128]{2,0,1:T(8,128)(2,1)S(1)}, bf16[16,1,128]{2,0,1:T(8,128)(2,1)S(1)}, u32[]{:S(2)}, u32[]{:S(2)}) collective-permute-start(bf16[16,1,128]{2,0,1:T(8,128)(2,1)S(1)} %slice.48), channel_id=1, source_target_pairs={{4,0},{8,4},{12,8},{16,12},{20,16},{24,20},{28,24},{32,28},{36,32}... | collective-permute-start | bytes 12296 | tf_op jit(solution)/shard_map/ppermute | solution.py:19
  40.8 216.5 %all-to-all-start.2 = ((bf16[64,4,3072]{2,0,1:T(8,128)(2,1)}), bf16[64,4,3072]{2,0,1:T(8,128)(2,1)}, u32[]{:S(2)}, u32[]{:S(2)}) async-start(bf16[64,4,3072]{2,0,1:T(8,128)(2,1)} %bitcast.225), calls=%async_computation.2 | async-start | bytes 3145728 | tf_op jit(solution)/shard_map/all_to_all | solution.py:152
  143.6 201.2 %collective-permute-start.4 = (bf16[256,1,192]{0,2,1:T(8,128)(2,1)}, bf16[256,1,192]{0,2,1:T(8,128)(2,1)}, u32[]{:S(2)}, u32[]{:S(2)}) collective-permute-start(bf16[256,1,192]{0,2,1:T(8,128)(2,1)} %copy.66), channel_id=1, source_target_pairs={{0,8},{4,12},{8,16},{12,20},{16,24},{20,28},{24,32},{28,36},{32,40... | collective-permute-start | bytes 294920 | tf_op jit(solution)/shard_map/ppermute | solution.py:19
  145.7 199.1 %collective-permute-start.5 = (bf16[256,1,192]{0,2,1:T(8,128)(2,1)}, bf16[256,1,192]{0,2,1:T(8,128)(2,1)}, u32[]{:S(2)}, u32[]{:S(2)}) collective-permute-start(bf16[256,1,192]{0,2,1:T(8,128)(2,1)} %copy.66), channel_id=1, source_target_pairs={{0,4},{4,8},{8,12},{12,16},{16,20},{20,24},{24,28},{28,32},{32,36}... | collective-permute-start | bytes 294920 | tf_op jit(solution)/shard_map/ppermute | solution.py:19
  148.5 5.0 %collective-permute-start = (bf16[16,1,192]{2,0,1:T(8,128)(2,1)S(1)}, bf16[16,1,192]{2,0,1:T(8,128)(2,1)S(1)}, u32[]{:S(2)}, u32[]{:S(2)}) collective-permute-start(bf16[16,1,192]{2,0,1:T(8,128)(2,1)S(1)} %slice.47), channel_id=1, source_target_pairs={{4,0},{8,4},{12,8},{16,12},{20,16},{24,20},{28,24},{32,28},{36,32}... | collective-permute-start | bytes 18440 | tf_op jit(solution)/shard_map/ppermute | solution.py:19
  257.3 9.1 %copy-start.4 = (f32[256,1,16]{0,2,1:T(8,128)S(1)}, f32[256,1,16]{0,2,1:T(8,128)}, u32[]{:S(2)}) copy-start(f32[256,1,16]{0,2,1:T(8,128)} %custom-call.1) | copy-start | bytes 49156
  266.4 78.4 %copy-start.2 = (pred[256,768]{0,1:T(8,128)(4,1)S(1)}, pred[256,768]{0,1:T(8,128)(4,1)}, u32[]{:S(2)}) copy-start(pred[256,768]{0,1:T(8,128)(4,1)} %and_and_fusion) | copy-start | bytes 589828
  270.8 3.8 %copy-start.1 = (f32[256,256,16]{1,0,2:T(8,128)S(1)}, f32[256,256,16]{1,0,2:T(8,128)}, u32[]{:S(2)}) copy-start(f32[256,256,16]{1,0,2:T(8,128)} %get-tuple-element.420) | copy-start | bytes 12582916 | tf_op jit(solution)/shard_map/while
  280.1 3.8 %copy-start.1 = (f32[256,256,16]{1,0,2:T(8,128)S(1)}, f32[256,256,16]{1,0,2:T(8,128)}, u32[]{:S(2)}) copy-start(f32[256,256,16]{1,0,2:T(8,128)} %get-tuple-element.420) | copy-start | bytes 12582916 | tf_op jit(solution)/shard_map/while
  289.3 3.8 %copy-start.1 = (f32[256,256,16]{1,0,2:T(8,128)S(1)}, f32[256,256,16]{1,0,2:T(8,128)}, u32[]{:S(2)}) copy-start(f32[256,256,16]{1,0,2:T(8,128)} %get-tuple-element.420) | copy-start | bytes 12582916 | tf_op jit(solution)/shard_map/while
  298.5 3.8 %copy-start.1 = (f32[256,256,16]{1,0,2:T(8,128)S(1)}, f32[256,256,16]{1,0,2:T(8,128)}, u32[]{:S(2)}) copy-start(f32[256,256,16]{1,0,2:T(8,128)} %get-tuple-element.420) | copy-start | bytes 12582916 | tf_op jit(solution)/shard_map/while
  307.7 3.8 %copy-start.1 = (f32[256,256,16]{1,0,2:T(8,128)S(1)}, f32[256,256,16]{1,0,2:T(8,128)}, u32[]{:S(2)}) copy-start(f32[256,256,16]{1,0,2:T(8,128)} %get-tuple-element.420) | copy-start | bytes 12582916 | tf_op jit(solution)/shard_map/while
  316.9 3.8 %copy-start.1 = (f32[256,256,16]{1,0,2:T(8,128)S(1)}, f32[256,256,16]{1,0,2:T(8,128)}, u32[]{:S(2)}) copy-start(f32[256,256,16]{1,0,2:T(8,128)} %get-tuple-element.420) | copy-start | bytes 12582916 | tf_op jit(solution)/shard_map/while
  326.1 3.8 %copy-start.1 = (f32[256,256,16]{1,0,2:T(8,128)S(1)}, f32[256,256,16]{1,0,2:T(8,128)}, u32[]{:S(2)}) copy-start(f32[256,256,16]{1,0,2:T(8,128)} %get-tuple-element.420) | copy-start | bytes 12582916 | tf_op jit(solution)/shard_map/while
  335.3 3.8 %copy-start.1 = (f32[256,256,16]{1,0,2:T(8,128)S(1)}, f32[256,256,16]{1,0,2:T(8,128)}, u32[]{:S(2)}) copy-start(f32[256,256,16]{1,0,2:T(8,128)} %get-tuple-element.420) | copy-start | bytes 12582916 | tf_op jit(solution)/shard_map/while
  349.5 2.6 copy-start.3
  349.5 2.6 copy-start.5
  349.5 2.6 copy-start.6
where the time goes:
time: 379 us; the launch traced here: 378 us
  blocking collectives  218 us (58%)
  matrix products  74.6 us (20%)
  starting transfers between devices  36.6 us (10%)
  local copies, waits for them, and re-layouts  28.1 us (7%)
  other arithmetic  13.2 us (3%)
  waiting for transfers between devices  6.88 us (2%)
    all_gather x1, blocking collectives, attend(): lax.all_gather(summary_keys, 'ctx', axis=0, tiled=True)  102 us
    all_gather x1, blocking collectives, attend(): lax.all_gather(summary_values, 'ctx', axis=0, tiled=True)  96.4 us
    dot_general x8, matrix products, absorb_part(): jnp.einsum('tghd,bgd->tghb', queried, part_keys, preferred_element_type=j...  34.3 us
    dot_general x8, matrix products, absorb_part(): jnp.einsum('tghb,bgd->tghd', weights.astype(jnp.bfloat16), part_values, p...  30.6 us
    ppermute x6, starting transfers between devices, passed_along(): lax.ppermute(value, axis, [(source, source + steps) for source in range(l...  19.7 us
    all_to_all x1, blocking collectives, local(): lax.all_to_all(mixture, 'head', split_axis=0, concat_axis=1, tiled=True)  19.2 us
    unnamed x18, local copies, waits for them, and re-layouts  8.06 us
  transfers between devices with their start and end apart: 10, of which 2 were waited for; matrix products, arithmetic and copies ran while one was open for 28% of the time, Pallas kernels for 0%

commit v1 on v0

--- a/solution.py
+++ b/solution.py
@@ -128,7 +128,9 @@
         jnp.zeros((row_count, group_count, per_group, VDIM), jnp.float32),
     )
     portion = (
-        lax.all_gather(summary_keys, "ctx", axis=0, tiled=True),
+        jnp.concatenate(
+            lax.all_to_all(jnp.stack([summary_keys] * lax.axis_size("ctx")), "ctx", 0, 0), axis=0
+        ),
         lax.all_gather(summary_values, "ctx", axis=0, tiled=True),
     )
     part_count = portion[0].shape[0]

time: 379 us -> 354 us (0.934)
  blocking collectives: 218 us -> 129 us
  starting transfers between devices: 36.6 us -> 68.6 us
  local copies, waits for them, and re-layouts: 28.1 us -> 46.2 us
  other arithmetic: 13.2 us -> 19.5 us
  matrix products: 74.6 us -> 78.8 us
    all_gather x1 -> x0, blocking collectives: 102 us -> none  [attend(): lax.all_gather(summary_keys, 'ctx', axis=0, tiled=True)]
    all_to_all x0 -> x1, starting transfers between devices: none -> 27.2 us  [attend(): lax.all_to_all(jnp.stack([summary_keys] * lax.axis_size('ctx')), 'ctx', 0...]
    all_gather x1, blocking collectives: 96.4 us -> 112 us  [attend(): lax.all_gather(summary_values, 'ctx', axis=0, tiled=True)]
    ppermute x6, starting transfers between devices: 19.7 us -> 25.5 us  [passed_along(): lax.ppermute(value, axis, [(source, source + steps) for source in range(l...]
    while x24 -> x56, local copies, waits for them, and re-layouts: 0.06 us -> 4.69 us
    unnamed x18 -> x20, local copies, waits for them, and re-layouts: 8.06 us -> 11.9 us
  transfers between devices with their start and end apart: 10 -> 11, of which waited for: 2 -> 5; matrix products, arithmetic and copies ran while one was open for 28% -> 35% of each run, Pallas kernels for 0% -> 0%
where the time goes in v1:
time: 354 us; the launch traced here: 352 us
  blocking collectives  129 us (36%)
  matrix products  78.8 us (22%)
  starting transfers between devices  68.6 us (19%)
  local copies, waits for them, and re-layouts  46.2 us (13%)
  other arithmetic  19.5 us (6%)
  waiting for transfers between devices  8.8 us (2%)
    all_gather x1, blocking collectives, attend(): lax.all_gather(summary_values, 'ctx', axis=0, tiled=True)  112 us
    dot_general x8, matrix products, absorb_part(): jnp.einsum('tghd,bgd->tghb', queried, part_keys, preferred_element_type=j...  34.1 us
    dot_general x8, matrix products, absorb_part(): jnp.einsum('tghb,bgd->tghd', weights.astype(jnp.bfloat16), part_values, p...  30.6 us
    all_to_all x1, starting transfers between devices, attend(): lax.all_to_all(jnp.stack([summary_keys] * lax.axis_size('ctx')), 'ctx', 0...  27.2 us
    ppermute x6, starting transfers between devices, passed_along(): lax.ppermute(value, axis, [(source, source + steps) for source in range(l...  25.5 us
    all_to_all x1, blocking collectives, local(): lax.all_to_all(mixture, 'head', split_axis=0, concat_axis=1, tiled=True)  17.3 us
    unnamed x20, local copies, waits for them, and re-layouts  11.9 us
    dot_general x1, matrix products, soft_mix(): jnp.einsum('tghs,sgd->tghd', weights.astype(jnp.bfloat16), value_rows, pr...  7.54 us
  transfers between devices with their start and end apart: 11, of which 5 were waited for; matrix products, arithmetic and copies ran while one was open for 35% of the time, Pallas kernels for 0%

profile of v1, /device:TPU:1, one launch (start us, length us, event | category | flops | bytes accessed | tf_op | source)
XLA Modules:
  0.0 352.2 jit_solution(1105776682521873866)
XLA Ops:
  0.0 0.9 copy.55
  1.6 4.8 %all-to-all-start = ((bf16[4,2,1024]{2,1,0:T(2,128)(2,1)}), bf16[4,2,1024]{2,1,0:T(2,128)(2,1)S(1)}, u32[]{:S(2)}, u32[]{:S(2)}) async-start(bf16[4,2,1024]{2,1,0:T(2,128)(2,1)} %reshape.428), calls=%async_computation | async-start | bytes 32768 | tf_op jit(solution)/shard_map/all_to_all | solution.py:157
  6.4 1.5 copy_bitcast_fusion.1
  7.9 2.7 all-to-all-done
  11.3 3.3 all-to-all-start.4
  14.5 1.1 all_to_all.65
  16.3 2.7 all-to-all-done.4
  19.0 3.3 all-to-all-start.1
  22.3 2.7 copy.125
  25.0 2.1 all-to-all-done.1
  27.1 4.4 %all-to-all-start.3 = ((bf16[64,4,3072]{2,0,1:T(8,128)(2,1)}), bf16[64,4,3072]{2,0,1:T(8,128)(2,1)}, u32[]{:S(2)}, u32[]{:S(2)}) async-start(bf16[64,4,3072]{2,0,1:T(8,128)(2,1)} %bitcast.203), calls=%async_computation.3 | async-start | bytes 3145728 | tf_op jit(solution)/shard_map/all_to_all | solution.py:154
  32.3 0.9 and_and_fusion
  33.3 10.6 %collective-permute-start = (bf16[16,1,192]{2,0,1:T(8,128)(2,1)S(1)}, bf16[16,1,192]{2,0,1:T(8,128)(2,1)S(1)}, u32[]{:S(2)}, u32[]{:S(2)}) collective-permute-start(bf16[16,1,192]{2,0,1:T(8,128)(2,1)S(1)} %slice.47), channel_id=1, source_target_pairs={{4,0},{8,4},{12,8},{16,12},{20,16},{24,20},{28,24},{32,28},{36,32}... | collective-permute-start | bytes 18440 | tf_op jit(solution)/shard_map/ppermute | solution.py:19
  45.1 1.0 stack.2
  46.1 27.2 %all-to-all-start.2 = ((bf16[128,16,1,192]{3,1,2,0:T(8,128)(2,1)}), bf16[128,16,1,192]{3,1,2,0:T(8,128)(2,1)S(1)}, u32[]{:S(2)}, u32[]{:S(2)}) async-start(bf16[128,16,1,192]{3,1,2,0:T(8,128)(2,1)} %stack.2), calls=%async_computation.2 | async-start | bytes 2097152 | tf_op jit(solution)/shard_map/all_to_all | solution.py:132
  73.3 1.3 fusion.63
  74.6 1.4 reshape.429
  77.5 1.5 reshape.411
  80.6 1.3 slice.48
  81.8 1.6 copy.63
  83.4 3.9 %collective-permute-start.2 = (bf16[256,1,128]{0,2,1:T(8,128)(2,1)}, bf16[256,1,128]{0,2,1:T(8,128)(2,1)}, u32[]{:S(2)}, u32[]{:S(2)}) collective-permute-start(bf16[256,1,128]{0,2,1:T(8,128)(2,1)} %copy.63), channel_id=1, source_target_pairs={{0,8},{4,12},{8,16},{12,20},{16,24},{20,28},{24,32},{28,36},{32,40... | collective-permute-start | bytes 196616 | tf_op jit(solution)/shard_map/ppermute | solution.py:19
  87.3 3.0 collective-permute-start.3
  90.3 1.9 collective-permute-start.1
  92.3 1.5 multiply_reduce_fusion.3
  93.7 1.4 copy.94
  96.6 1.3 multiply_reduce_fusion.2
  97.9 1.4 copy.101
  99.4 1.7 fusion.43
  101.0 1.7 copy.66
  102.7 3.4 collective-permute-start.4
  106.1 2.7 collective-permute-start.5
  108.8 112.0 %all_gather.3 = bf16[2048,1,128]{2,0,1:T(8,128)(2,1)} all-gather(bf16[16,1,128]{2,0,1:T(8,128)(2,1)} %fusion.43), channel_id=1, replica_groups=mesh['ctx'=128,'head'=4] {'ctx'}, dimensions={0}, use_global_device_ids=true | all-gather | bytes 528384 | tf_op jit(solution)/shard_map/all_gather | solution.py:134
  220.8 4.8 %reshape.398 = bf16[256,1,16,192]{3,2,0,1:T(8,128)(2,1)} reshape(bf16[4,64,3072]{2,1,0:T(8,128)(2,1)} %bitcast.30) | data formatting | bytes 3145728 | tf_op jit(solution)/shard_map/reshape | solution.py:68
  225.6 4.7 %reshape.408 = bf16[256,16,192]{2,1,0:T(8,128)(2,1)} reshape(bf16[4,64,3072]{2,1,0:T(8,128)(2,1)} %bitcast.30) | data formatting | bytes 3145728 | tf_op jit(solution)/shard_map/reshape.40
  230.3 4.5 %copy.61 = bf16[256,1,16,192]{0,3,2,1:T(8,128)(2,1)} copy(bf16[256,1,16,192]{3,2,0,1:T(8,128)(2,1)} %reshape.398) | data formatting | bytes 3145728
  234.8 4.7 %fusion.27 = (f32[256,16]{0,1:T(8,128)S(1)}, f32[768,256,16]{1,0,2:T(8,128)S(1)}) fusion(pred[256,768]{0,1:T(8,128)(4,1)} %and_and_fusion, bf16[256,16,192]{2,1,0:T(8,128)(2,1)} %reshape.408, bf16[256,1,192]{0,2,1:T(8,128)(2,1)} %copy.66, bf16[256,1,192]{0,2,1:T(8,128)(2,1)} %collective-permute-done.5, bf16[256,1,192]{0,2,1:T(8,128)(2,1)} %collective-permute-done.4), kind=kOutput, calls=%fused_computation.36 | convolution fusion | flops 1218277376 | bytes 14663680 | tf_op jit(solution)/shard_map/tghd,sgd->tghs/dot_general | solution.py:98
  239.5 2.5 fusion.30
  242.0 2.0 copy-done.2
  244.6 1.2 copy.60
  245.8 78.2 %while.22 = (s32[]{:T(128)}, f32[256,1,16]{0,2,1:T(8,128)S(1)}, f32[256,1,16]{0,2,1:T(8,128)}, f32[256,1,16,128]{0,3,2,1:T(8,128)S(1)}, bf16[2048,1,192]{0,2,1:T...) while((s32[]{:T(128)}, f32[256,1,16]{0,2,1:T(8,128)S(1)}, ...), condition=%wide.region_3.4_spmd.clone, body=%wide.region_0.3_spmd.clone.sunk | while | flops 684286976 | bytes 35950864 | solution.py:143
  246.0 4.3 %fusion.80 = (f32[256,16]{0,1:T(8,128)S(1)}, f32[256,256,16]{1,0,2:T(8,128)}) fusion(pred[256,256]{0,1:T(8,128)(4,1)S(1)} %broadcast_compare_fusion.3, bf16[256,1,16,192]{0,3,2,1:T(8,128)(2,1)} %get-tuple-element.451, bf16[2048,1,192]{0,2,1:T(8,128)(2,1)} %get-tuple-element.450, s32[]{:T(128)S(6)} %select_n.112), kind=kOutput, calls=%fused_computation.3.clone.1 | convolution fusion | flops 405794816 | bytes 5947396 | tf_op jit(solution)/shard_map/while/body/eval_jaxpr/tghd,bgd->tghb/dot_general | solution.py:109
  250.3 3.8 %bitcast_add_fusion.6 = f32[256,1,16,128]{0,3,2,1:T(8,128)S(1)} fusion(f32[256,1,16,128]{0,3,2,1:T(8,128)S(1)} %get-tuple-element.437, f32[256,256,16]{1,0,2:T(8,128)} %get-tuple-element.420, f32[256,16]{0,1:T(8,128)S(1)} %bitcast.226, pred[256,256]{0,1:T(8,128)(4,1)S(1)} %broadcast_compare_fusion.3, f32[256,16]{0,1:T(8,128)S(1)} %get-tuple-element.421, ...), kind=kOutput, calls=%fused_computation.10.clone.1 | convolution fusion | flops 274202624 | bytes 8552453 | tf_op jit(solution)/shard_map/while/body/eval_jaxpr/tghb,bgd->tghd/dot_general | solution.py:117
  254.1 0.9 fusion.82
  255.7 4.3 %fusion.80 = (f32[256,16]{0,1:T(8,128)S(1)}, f32[256,256,16]{1,0,2:T(8,128)}) fusion(pred[256,256]{0,1:T(8,128)(4,1)S(1)} %broadcast_compare_fusion.3, bf16[256,1,16,192]{0,3,2,1:T(8,128)(2,1)} %get-tuple-element.451, bf16[2048,1,192]{0,2,1:T(8,128)(2,1)} %get-tuple-element.450, s32[]{:T(128)S(6)} %select_n.112), kind=kOutput, calls=%fused_computation.3.clone.1 | convolution fusion | flops 405794816 | bytes 5947396 | tf_op jit(solution)/shard_map/while/body/eval_jaxpr/tghd,bgd->tghb/dot_general | solution.py:109
  260.0 3.8 %bitcast_add_fusion.6 = f32[256,1,16,128]{0,3,2,1:T(8,128)S(1)} fusion(f32[256,1,16,128]{0,3,2,1:T(8,128)S(1)} %get-tuple-element.437, f32[256,256,16]{1,0,2:T(8,128)} %get-tuple-element.420, f32[256,16]{0,1:T(8,128)S(1)} %bitcast.226, pred[256,256]{0,1:T(8,128)(4,1)S(1)} %broadcast_compare_fusion.3, f32[256,16]{0,1:T(8,128)S(1)} %get-tuple-element.421, ...), kind=kOutput, calls=%fused_computation.10.clone.1 | convolution fusion | flops 274202624 | bytes 8552453 | tf_op jit(solution)/shard_map/while/body/eval_jaxpr/tghb,bgd->tghd/dot_general | solution.py:117
  263.9 0.9 fusion.82
  265.5 4.3 %fusion.80 = (f32[256,16]{0,1:T(8,128)S(1)}, f32[256,256,16]{1,0,2:T(8,128)}) fusion(pred[256,256]{0,1:T(8,128)(4,1)S(1)} %broadcast_compare_fusion.3, bf16[256,1,16,192]{0,3,2,1:T(8,128)(2,1)} %get-tuple-element.451, bf16[2048,1,192]{0,2,1:T(8,128)(2,1)} %get-tuple-element.450, s32[]{:T(128)S(6)} %select_n.112), kind=kOutput, calls=%fused_computation.3.clone.1 | convolution fusion | flops 405794816 | bytes 5947396 | tf_op jit(solution)/shard_map/while/body/eval_jaxpr/tghd,bgd->tghb/dot_general | solution.py:109
  269.8 3.8 %bitcast_add_fusion.6 = f32[256,1,16,128]{0,3,2,1:T(8,128)S(1)} fusion(f32[256,1,16,128]{0,3,2,1:T(8,128)S(1)} %get-tuple-element.437, f32[256,256,16]{1,0,2:T(8,128)} %get-tuple-element.420, f32[256,16]{0,1:T(8,128)S(1)} %bitcast.226, pred[256,256]{0,1:T(8,128)(4,1)S(1)} %broadcast_compare_fusion.3, f32[256,16]{0,1:T(8,128)S(1)} %get-tuple-element.421, ...), kind=kOutput, calls=%fused_computation.10.clone.1 | convolution fusion | flops 274202624 | bytes 8552453 | tf_op jit(solution)/shard_map/while/body/eval_jaxpr/tghb,bgd->tghd/dot_general | solution.py:117
  273.6 0.9 fusion.82
  275.3 4.3 %fusion.80 = (f32[256,16]{0,1:T(8,128)S(1)}, f32[256,256,16]{1,0,2:T(8,128)}) fusion(pred[256,256]{0,1:T(8,128)(4,1)S(1)} %broadcast_compare_fusion.3, bf16[256,1,16,192]{0,3,2,1:T(8,128)(2,1)} %get-tuple-element.451, bf16[2048,1,192]{0,2,1:T(8,128)(2,1)} %get-tuple-element.450, s32[]{:T(128)S(6)} %select_n.112), kind=kOutput, calls=%fused_computation.3.clone.1 | convolution fusion | flops 405794816 | bytes 5947396 | tf_op jit(solution)/shard_map/while/body/eval_jaxpr/tghd,bgd->tghb/dot_general | solution.py:109
  279.6 3.8 %bitcast_add_fusion.6 = f32[256,1,16,128]{0,3,2,1:T(8,128)S(1)} fusion(f32[256,1,16,128]{0,3,2,1:T(8,128)S(1)} %get-tuple-element.437, f32[256,256,16]{1,0,2:T(8,128)} %get-tuple-element.420, f32[256,16]{0,1:T(8,128)S(1)} %bitcast.226, pred[256,256]{0,1:T(8,128)(4,1)S(1)} %broadcast_compare_fusion.3, f32[256,16]{0,1:T(8,128)S(1)} %get-tuple-element.421, ...), kind=kOutput, calls=%fused_computation.10.clone.1 | convolution fusion | flops 274202624 | bytes 8552453 | tf_op jit(solution)/shard_map/while/body/eval_jaxpr/tghb,bgd->tghd/dot_general | solution.py:117
  283.4 0.9 fusion.82
  285.0 4.3 %fusion.80 = (f32[256,16]{0,1:T(8,128)S(1)}, f32[256,256,16]{1,0,2:T(8,128)}) fusion(pred[256,256]{0,1:T(8,128)(4,1)S(1)} %broadcast_compare_fusion.3, bf16[256,1,16,192]{0,3,2,1:T(8,128)(2,1)} %get-tuple-element.451, bf16[2048,1,192]{0,2,1:T(8,128)(2,1)} %get-tuple-element.450, s32[]{:T(128)S(6)} %select_n.112), kind=kOutput, calls=%fused_computation.3.clone.1 | convolution fusion | flops 405794816 | bytes 5947396 | tf_op jit(solution)/shard_map/while/body/eval_jaxpr/tghd,bgd->tghb/dot_general | solution.py:109
  289.3 3.8 %bitcast_add_fusion.6 = f32[256,1,16,128]{0,3,2,1:T(8,128)S(1)} fusion(f32[256,1,16,128]{0,3,2,1:T(8,128)S(1)} %get-tuple-element.437, f32[256,256,16]{1,0,2:T(8,128)} %get-tuple-element.420, f32[256,16]{0,1:T(8,128)S(1)} %bitcast.226, pred[256,256]{0,1:T(8,128)(4,1)S(1)} %broadcast_compare_fusion.3, f32[256,16]{0,1:T(8,128)S(1)} %get-tuple-element.421, ...), kind=kOutput, calls=%fused_computation.10.clone.1 | convolution fusion | flops 274202624 | bytes 8552453 | tf_op jit(solution)/shard_map/while/body/eval_jaxpr/tghb,bgd->tghd/dot_general | solution.py:117
  294.8 4.3 %fusion.80 = (f32[256,16]{0,1:T(8,128)S(1)}, f32[256,256,16]{1,0,2:T(8,128)}) fusion(pred[256,256]{0,1:T(8,128)(4,1)S(1)} %broadcast_compare_fusion.3, bf16[256,1,16,192]{0,3,2,1:T(8,128)(2,1)} %get-tuple-element.451, bf16[2048,1,192]{0,2,1:T(8,128)(2,1)} %get-tuple-element.450, s32[]{:T(128)S(6)} %select_n.112), kind=kOutput, calls=%fused_computation.3.clone.1 | convolution fusion | flops 405794816 | bytes 5947396 | tf_op jit(solution)/shard_map/while/body/eval_jaxpr/tghd,bgd->tghb/dot_general | solution.py:109
  299.1 3.8 %bitcast_add_fusion.6 = f32[256,1,16,128]{0,3,2,1:T(8,128)S(1)} fusion(f32[256,1,16,128]{0,3,2,1:T(8,128)S(1)} %get-tuple-element.437, f32[256,256,16]{1,0,2:T(8,128)} %get-tuple-element.420, f32[256,16]{0,1:T(8,128)S(1)} %bitcast.226, pred[256,256]{0,1:T(8,128)(4,1)S(1)} %broadcast_compare_fusion.3, f32[256,16]{0,1:T(8,128)S(1)} %get-tuple-element.421, ...), kind=kOutput, calls=%fused_computation.10.clone.1 | convolution fusion | flops 274202624 | bytes 8552453 | tf_op jit(solution)/shard_map/while/body/eval_jaxpr/tghb,bgd->tghd/dot_general | solution.py:117
  304.6 4.3 %fusion.80 = (f32[256,16]{0,1:T(8,128)S(1)}, f32[256,256,16]{1,0,2:T(8,128)}) fusion(pred[256,256]{0,1:T(8,128)(4,1)S(1)} %broadcast_compare_fusion.3, bf16[256,1,16,192]{0,3,2,1:T(8,128)(2,1)} %get-tuple-element.451, bf16[2048,1,192]{0,2,1:T(8,128)(2,1)} %get-tuple-element.450, s32[]{:T(128)S(6)} %select_n.112), kind=kOutput, calls=%fused_computation.3.clone.1 | convolution fusion | flops 405794816 | bytes 5947396 | tf_op jit(solution)/shard_map/while/body/eval_jaxpr/tghd,bgd->tghb/dot_general | solution.py:109
  308.9 3.8 %bitcast_add_fusion.6 = f32[256,1,16,128]{0,3,2,1:T(8,128)S(1)} fusion(f32[256,1,16,128]{0,3,2,1:T(8,128)S(1)} %get-tuple-element.437, f32[256,256,16]{1,0,2:T(8,128)} %get-tuple-element.420, f32[256,16]{0,1:T(8,128)S(1)} %bitcast.226, pred[256,256]{0,1:T(8,128)(4,1)S(1)} %broadcast_compare_fusion.3, f32[256,16]{0,1:T(8,128)S(1)} %get-tuple-element.421, ...), kind=kOutput, calls=%fused_computation.10.clone.1 | convolution fusion | flops 274202624 | bytes 8552453 | tf_op jit(solution)/shard_map/while/body/eval_jaxpr/tghb,bgd->tghd/dot_general | solution.py:117
  314.3 4.3 %fusion.80 = (f32[256,16]{0,1:T(8,128)S(1)}, f32[256,256,16]{1,0,2:T(8,128)}) fusion(pred[256,256]{0,1:T(8,128)(4,1)S(1)} %broadcast_compare_fusion.3, bf16[256,1,16,192]{0,3,2,1:T(8,128)(2,1)} %get-tuple-element.451, bf16[2048,1,192]{0,2,1:T(8,128)(2,1)} %get-tuple-element.450, s32[]{:T(128)S(6)} %select_n.112), kind=kOutput, calls=%fused_computation.3.clone.1 | convolution fusion | flops 405794816 | bytes 5947396 | tf_op jit(solution)/shard_map/while/body/eval_jaxpr/tghd,bgd->tghb/dot_general | solution.py:109
  318.6 3.8 %bitcast_add_fusion.6 = f32[256,1,16,128]{0,3,2,1:T(8,128)S(1)} fusion(f32[256,1,16,128]{0,3,2,1:T(8,128)S(1)} %get-tuple-element.437, f32[256,256,16]{1,0,2:T(8,128)} %get-tuple-element.420, f32[256,16]{0,1:T(8,128)S(1)} %bitcast.226, pred[256,256]{0,1:T(8,128)(4,1)S(1)} %broadcast_compare_fusion.3, f32[256,16]{0,1:T(8,128)S(1)} %get-tuple-element.421, ...), kind=kOutput, calls=%fused_computation.10.clone.1 | convolution fusion | flops 274202624 | bytes 8552453 | tf_op jit(solution)/shard_map/while/body/eval_jaxpr/tghb,bgd->tghd/dot_general | solution.py:117
  324.7 7.5 %fusion.36 = bf16[256,1,16,128]{0,3,2,1:T(8,128)(2,1)S(1)} fusion(f32[256,1,16,128]{0,3,2,1:T(8,128)S(1)} %get-tuple-element.263, f32[768,256,16]{1,0,2:T(8,128)} %copy-done.2, f32[256,16]{0,1:T(8,128)} %copy-done.9, pred[256,768]{0,1:T(8,128)(4,1)} %and_and_fusion, f32[256,16]{0,1:T(8,128)} %compare_select_fusion, f32[256,16]{0,1:T(8,128)} %get-tuple-element.359, ...), kind=kOutput, calls=%fused_computation.45 | convolution fusion | flops 821624832 | bytes 16203776 | tf_op jit(solution)/shard_map/tghs,sgd->tghd/dot_general | solution.py:42
  332.3 1.1 copy.71
  333.9 17.3 %all_to_all.85 = bf16[4,64,2048]{2,1,0:T(8,128)(2,1)S(1)} all-to-all(bf16[4,64,2048]{2,1,0:T(8,128)(2,1)S(1)} %all_to_all.75), channel_id=1, replica_groups=mesh['ctx'=128,'head'=4] {'head'}, dimensions={0} | all-to-all | bytes 2097152 | tf_op jit(solution)/shard_map/all_to_all | solution.py:178
  351.2 1.0 copy.116
  (137 shorter events, 19.4 us)
Async XLA Ops:
  0.0 44.9 %copy-start = (bf16[4,192,192]{2,1,0:T(8,128)(2,1)S(1)}, bf16[4,192,192]{2,1,0:T(8,128)(2,1)}, u32[]{:S(2)}) copy-start(bf16[4,192,192]{2,1,0:T(8,128)(2,1)} %param.15) | copy-start | bytes 884740
  1.6 9.1 %all-to-all-start = ((bf16[4,2,1024]{2,1,0:T(2,128)(2,1)}), bf16[4,2,1024]{2,1,0:T(2,128)(2,1)S(1)}, u32[]{:S(2)}, u32[]{:S(2)}) async-start(bf16[4,2,1024]{2,1,0:T(2,128)(2,1)} %reshape.428), calls=%async_computation | async-start | bytes 32768 | tf_op jit(solution)/shard_map/all_to_all | solution.py:157
  10.7 0.6 copy-start.8
  11.3 7.7 %all-to-all-start.4 = ((bf16[64,4,128]{2,0,1:T(8,128)(2,1)}), bf16[64,4,128]{2,0,1:T(8,128)(2,1)S(1)}, u32[]{:S(2)}, u32[]{:S(2)}) async-start(bf16[64,4,128]{2,0,1:T(8,128)(2,1)} %copy_bitcast_fusion.1), calls=%async_computation.4 | async-start | bytes 131072 | tf_op jit(solution)/shard_map/all_to_all | solution.py:156
  19.0 12.5 %copy-start.4 = (bf16[64,4,128]{2,0,1:T(8,128)(2,1)}, bf16[64,4,128]{2,0,1:T(8,128)(2,1)S(1)}, u32[]{:S(2)}) copy-start(bf16[64,4,128]{2,0,1:T(8,128)(2,1)S(1)} %all-to-all-done.4) | copy-start | bytes 196612
  19.0 8.1 %all-to-all-start.1 = ((bf16[64,4,192]{2,0,1:T(8,128)(2,1)}), bf16[64,4,192]{2,0,1:T(8,128)(2,1)S(1)}, u32[]{:S(2)}, u32[]{:S(2)}) async-start(bf16[64,4,192]{2,0,1:T(8,128)(2,1)} %copy.57), calls=%async_computation.1 | async-start | bytes 262144 | tf_op jit(solution)/shard_map/all_to_all | solution.py:155
  27.1 19.0 %copy-start.3 = (bf16[64,4,192]{2,0,1:T(8,128)(2,1)}, bf16[64,4,192]{2,0,1:T(8,128)(2,1)S(1)}, u32[]{:S(2)}) copy-start(bf16[64,4,192]{2,0,1:T(8,128)(2,1)S(1)} %all-to-all-done.1) | copy-start | bytes 294916
  27.1 17.9 %all-to-all-start.3 = ((bf16[64,4,3072]{2,0,1:T(8,128)(2,1)}), bf16[64,4,3072]{2,0,1:T(8,128)(2,1)}, u32[]{:S(2)}, u32[]{:S(2)}) async-start(bf16[64,4,3072]{2,0,1:T(8,128)(2,1)} %bitcast.203), calls=%async_computation.3 | async-start | bytes 3145728 | tf_op jit(solution)/shard_map/all_to_all | solution.py:154
  33.3 11.4 %collective-permute-start = (bf16[16,1,192]{2,0,1:T(8,128)(2,1)S(1)}, bf16[16,1,192]{2,0,1:T(8,128)(2,1)S(1)}, u32[]{:S(2)}, u32[]{:S(2)}) collective-permute-start(bf16[16,1,192]{2,0,1:T(8,128)(2,1)S(1)} %slice.47), channel_id=1, source_target_pairs={{4,0},{8,4},{12,8},{16,12},{20,16},{24,20},{28,24},{32,28},{36,32}... | collective-permute-start | bytes 18440 | tf_op jit(solution)/shard_map/ppermute | solution.py:19
  46.1 198.5 %all-to-all-start.2 = ((bf16[128,16,1,192]{3,1,2,0:T(8,128)(2,1)}), bf16[128,16,1,192]{3,1,2,0:T(8,128)(2,1)S(1)}, u32[]{:S(2)}, u32[]{:S(2)}) async-start(bf16[128,16,1,192]{3,1,2,0:T(8,128)(2,1)} %stack.2), calls=%async_computation.2 | async-start | bytes 2097152 | tf_op jit(solution)/shard_map/all_to_all | solution.py:132
  83.4 241.3 %collective-permute-start.2 = (bf16[256,1,128]{0,2,1:T(8,128)(2,1)}, bf16[256,1,128]{0,2,1:T(8,128)(2,1)}, u32[]{:S(2)}, u32[]{:S(2)}) collective-permute-start(bf16[256,1,128]{0,2,1:T(8,128)(2,1)} %copy.63), channel_id=1, source_target_pairs={{0,8},{4,12},{8,16},{12,20},{16,24},{20,28},{24,32},{28,36},{32,40... | collective-permute-start | bytes 196616 | tf_op jit(solution)/shard_map/ppermute | solution.py:19
  87.3 237.4 %collective-permute-start.3 = (bf16[256,1,128]{0,2,1:T(8,128)(2,1)}, bf16[256,1,128]{0,2,1:T(8,128)(2,1)}, u32[]{:S(2)}, u32[]{:S(2)}) collective-permute-start(bf16[256,1,128]{0,2,1:T(8,128)(2,1)} %copy.63), channel_id=1, source_target_pairs={{0,4},{4,8},{8,12},{12,16},{16,20},{20,24},{24,28},{28,32},{32,36}... | collective-permute-start | bytes 196616 | tf_op jit(solution)/shard_map/ppermute | solution.py:19
  90.3 5.4 %collective-permute-start.1 = (bf16[16,1,128]{2,0,1:T(8,128)(2,1)}, bf16[16,1,128]{2,0,1:T(8,128)(2,1)}, u32[]{:S(2)}, u32[]{:S(2)}) collective-permute-start(bf16[16,1,128]{2,0,1:T(8,128)(2,1)} %slice.48), channel_id=1, source_target_pairs={{4,0},{8,4},{12,8},{16,12},{20,16},{24,20},{28,24},{32,28},{36,32}... | collective-permute-start | bytes 12296 | tf_op jit(solution)/shard_map/ppermute | solution.py:19
  102.7 132.1 %collective-permute-start.4 = (bf16[256,1,192]{0,2,1:T(8,128)(2,1)}, bf16[256,1,192]{0,2,1:T(8,128)(2,1)}, u32[]{:S(2)}, u32[]{:S(2)}) collective-permute-start(bf16[256,1,192]{0,2,1:T(8,128)(2,1)} %copy.66), channel_id=1, source_target_pairs={{0,8},{4,12},{8,16},{12,20},{16,24},{20,28},{24,32},{28,36},{32,40... | collective-permute-start | bytes 294920 | tf_op jit(solution)/shard_map/ppermute | solution.py:19
  106.1 128.7 %collective-permute-start.5 = (bf16[256,1,192]{0,2,1:T(8,128)(2,1)}, bf16[256,1,192]{0,2,1:T(8,128)(2,1)}, u32[]{:S(2)}, u32[]{:S(2)}) collective-permute-start(bf16[256,1,192]{0,2,1:T(8,128)(2,1)} %copy.66), channel_id=1, source_target_pairs={{0,4},{4,8},{8,12},{12,16},{16,20},{20,24},{24,28},{28,32},{32,36}... | collective-permute-start | bytes 294920 | tf_op jit(solution)/shard_map/ppermute | solution.py:19
  234.8 4.7 %copy-start.5 = (pred[256,768]{0,1:T(8,128)(4,1)S(1)}, pred[256,768]{0,1:T(8,128)(4,1)}, u32[]{:S(2)}) copy-start(pred[256,768]{0,1:T(8,128)(4,1)} %and_and_fusion) | copy-start | bytes 589828
  239.5 4.5 %copy-start.2 = (f32[768,256,16]{1,0,2:T(8,128)}, f32[768,256,16]{1,0,2:T(8,128)S(1)}, u32[]{:S(2)}) copy-start(f32[768,256,16]{1,0,2:T(8,128)S(1)} %get-tuple-element.356) | copy-start | bytes 37748740
  239.5 4.5 %copy-start.9 = (f32[256,16]{0,1:T(8,128)}, f32[256,16]{0,1:T(8,128)S(1)}, u32[]{:S(2)}) copy-start(f32[256,16]{0,1:T(8,128)S(1)} %get-tuple-element.355) | copy-start | bytes 49156
  250.2 3.8 %copy-start.1 = (f32[256,256,16]{1,0,2:T(8,128)S(1)}, f32[256,256,16]{1,0,2:T(8,128)}, u32[]{:S(2)}) copy-start(f32[256,256,16]{1,0,2:T(8,128)} %get-tuple-element.420) | copy-start | bytes 12582916 | tf_op jit(solution)/shard_map/while
  254.1 0.9 copy-start.6
  255.0 0.6 copy-start.7
  260.0 3.8 %copy-start.1 = (f32[256,256,16]{1,0,2:T(8,128)S(1)}, f32[256,256,16]{1,0,2:T(8,128)}, u32[]{:S(2)}) copy-start(f32[256,256,16]{1,0,2:T(8,128)} %get-tuple-element.420) | copy-start | bytes 12582916 | tf_op jit(solution)/shard_map/while
  263.9 0.9 copy-start.6
  264.8 0.6 copy-start.7
  269.8 3.8 %copy-start.1 = (f32[256,256,16]{1,0,2:T(8,128)S(1)}, f32[256,256,16]{1,0,2:T(8,128)}, u32[]{:S(2)}) copy-start(f32[256,256,16]{1,0,2:T(8,128)} %get-tuple-element.420) | copy-start | bytes 12582916 | tf_op jit(solution)/shard_map/while
  273.6 0.9 copy-start.6
  274.5 0.6 copy-start.7
  279.5 3.8 %copy-start.1 = (f32[256,256,16]{1,0,2:T(8,128)S(1)}, f32[256,256,16]{1,0,2:T(8,128)}, u32[]{:S(2)}) copy-start(f32[256,256,16]{1,0,2:T(8,128)} %get-tuple-element.420) | copy-start | bytes 12582916 | tf_op jit(solution)/shard_map/while
  283.4 0.9 copy-start.6
  284.3 0.6 copy-start.7
  289.3 3.8 %copy-start.1 = (f32[256,256,16]{1,0,2:T(8,128)S(1)}, f32[256,256,16]{1,0,2:T(8,128)}, u32[]{:S(2)}) copy-start(f32[256,256,16]{1,0,2:T(8,128)} %get-tuple-element.420) | copy-start | bytes 12582916 | tf_op jit(solution)/shard_map/while
  293.2 0.9 copy-start.6
  294.1 0.6 copy-start.7
  299.1 3.8 %copy-start.1 = (f32[256,256,16]{1,0,2:T(8,128)S(1)}, f32[256,256,16]{1,0,2:T(8,128)}, u32[]{:S(2)}) copy-start(f32[256,256,16]{1,0,2:T(8,128)} %get-tuple-element.420) | copy-start | bytes 12582916 | tf_op jit(solution)/shard_map/while
  302.9 0.9 copy-start.6
  303.9 0.6 copy-start.7
  308.9 3.8 %copy-start.1 = (f32[256,256,16]{1,0,2:T(8,128)S(1)}, f32[256,256,16]{1,0,2:T(8,128)}, u32[]{:S(2)}) copy-start(f32[256,256,16]{1,0,2:T(8,128)} %get-tuple-element.420) | copy-start | bytes 12582916 | tf_op jit(solution)/shard_map/while
  312.7 0.9 copy-start.6
  313.6 0.6 copy-start.7
  318.6 3.8 %copy-start.1 = (f32[256,256,16]{1,0,2:T(8,128)S(1)}, f32[256,256,16]{1,0,2:T(8,128)}, u32[]{:S(2)}) copy-start(f32[256,256,16]{1,0,2:T(8,128)} %get-tuple-element.420) | copy-start | bytes 12582916 | tf_op jit(solution)/shard_map/while
  322.5 0.9 copy-start.6
  323.4 0.6 copy-start.7
